TPU v7x, 256 devices: a whole 4x4x8 slice. The times are simulated.
256 devices in a mesh: ctx: 32 (over x_hi, z, core), row: 4 (over y), col: 2 (over x_lo).
Axes of the slice: x: 4 (x_hi: 2, x_lo: 2; x = x_hi * 2 + x_lo), y: 4, z: 8, core: 2. Of those that a mesh axis runs over, the one named last changes fastest.
Arguments:
- inputs: bfloat16 [4096, 8192], P('ctx', ('row', 'col')), may hold values from -6 to 6
- queries: bfloat16 [4096, 8192], P('ctx', ('row', 'col')), may hold values from -16 to 16
- out_grad: bfloat16 [4096, 8192], P('ctx', ('row', 'col')), may hold values from -6 to 6
- w_key: bfloat16 [8192, 1024], P(('row', 'col')), may hold values from -0.0625 to 0.0625
- w_value: bfloat16 [8192, 1024], P(('row', 'col')), may hold values from -0.0625 to 0.0625
- key_bias: float32 [1024], replicated, may hold values from -16 to 16
- block_order: int32 [64], replicated, may hold values from 0 to 63, as said below
Outputs:
- grad_inputs: bfloat16 [4096, 8192], P('ctx', ('row', 'col'))
- grad_queries: bfloat16 [4096, 8192], P('ctx', ('row', 'col'))
- grad_w_key: bfloat16 [8192, 1024], P(('row', 'col'), 'ctx')
- grad_w_value: bfloat16 [8192, 1024], P(('row', 'col'), 'ctx')
- grad_key_bias: float32 [1024], P('ctx')
- grad_value_bias: float32 [1024], P('ctx')
Inputs may be any that keep to these rules, and one draw needn't show every extreme that they name: block_order is a permutation; storage blocks 2 c and 2 c + 1 hold sequence blocks a and 63 - a for some a < 32, in either order.
All inputs are finite; a program needn't handle non-finite values.
Results may differ from a plain program's by a relative error of at most 0.015.
The roundings to bfloat16 on the way count: a program that leaves them out, or rounds other values in their place, can miss the bound.
Values may be sent and summed in bfloat16 or wider, within the bound.
A program may use at most 64 MiB of HBM per device.

v0:
```python
import math

import jax
import jax.numpy as jnp
from jax import lax
from jax.sharding import PartitionSpec as P

HD = 128


ROPE_BASE = 1000000.0
MASKED = -1e30


def passed_along(block, axis, distance):
    devices = range(lax.axis_size(axis))
    route = [((i - distance) % len(devices), i) for i in devices]
    return lax.ppermute(block, axis, route)


def rope_tables(positions):
    half_width = HD // 2
    frequency = ROPE_BASE ** (-jnp.arange(half_width, dtype=jnp.float32) * 2.0 / HD)
    angles = positions.astype(jnp.float32)[:, None] * frequency[None, :]
    return (jnp.cos(angles), jnp.sin(angles))


def rotate(tensor, cosine_table, sine_table):
    half_width = tensor.shape[-1] // 2
    lower_part = tensor[..., :half_width]
    upper_part = tensor[..., half_width:]
    return jnp.concatenate(
        [
            lower_part * cosine_table - upper_part * sine_table,
            upper_part * cosine_table + lower_part * sine_table,
        ],
        axis=-1,
    )


def unrotate(tensor, cosine_table, sine_table):
    half_width = tensor.shape[-1] // 2
    lower_part = tensor[..., :half_width]
    upper_part = tensor[..., half_width:]
    return jnp.concatenate(
        [
            lower_part * cosine_table + upper_part * sine_table,
            upper_part * cosine_table - lower_part * sine_table,
        ],
        axis=-1,
    )


def own_positions(block_order, owner_index, tok_rows):
    pair_ids = lax.dynamic_slice_in_dim(block_order, 2 * owner_index, 2)
    half_block = tok_rows // 2
    lane_index = jnp.arange(tok_rows, dtype=jnp.int32)
    chosen = jnp.where(lane_index < half_block, pair_ids[0], pair_ids[1])
    return chosen * half_block + lane_index % half_block


def piece_positions(block_order, count_rows, half_block):
    row_ids = jnp.arange(count_rows, dtype=jnp.int32)
    slot_ids = jnp.arange(block_order.shape[0], dtype=jnp.int32)
    onehot = (row_ids // half_block)[:, None] == slot_ids[None, :]
    chosen = jnp.sum(jnp.where(onehot, block_order[None, :], 0), axis=1)
    return chosen * half_block + row_ids % half_block


def body(inputs, queries, out_grad, w_key, w_value, key_bias, block_order):
    cycle_size = lax.axis_size("ctx")
    ctx_index = lax.axis_index("ctx")
    head_index = lax.axis_index("row") * lax.axis_size("col") + lax.axis_index("col")
    tok_rows = inputs.shape[0]
    half_block = tok_rows // 2
    group_heads = queries.shape[1] // HD
    score_scale = HD ** (-0.5)
    own_pos = own_positions(block_order, ctx_index, tok_rows)
    cosine_table, sine_table = rope_tables(own_pos)
    part_key = jnp.dot(inputs, w_key, preferred_element_type=jnp.float32)
    part_value = jnp.dot(inputs, w_value, preferred_element_type=jnp.float32)
    sum_key, sum_value = (
        lax.psum_scatter(part_key, ("row", "col"), scatter_dimension=1, tiled=True),
        lax.psum_scatter(part_value, ("row", "col"), scatter_dimension=1, tiled=True),
    )
    key_pre = sum_key + lax.dynamic_slice_in_dim(key_bias, head_index * HD, HD)[None, :]
    head_keys = rotate(key_pre, cosine_table, sine_table).astype(jnp.bfloat16)
    head_values = sum_value.astype(jnp.bfloat16)
    query_rows = (
        queries.reshape(tok_rows, group_heads, HD)
        .transpose(1, 0, 2)
        .reshape(group_heads * tok_rows, HD)
    )
    grad_rows = (
        out_grad.reshape(tok_rows, group_heads, HD)
        .transpose(1, 0, 2)
        .reshape(group_heads * tok_rows, HD)
    )
    query_pos = jnp.tile(own_pos, group_heads)
    total_rows = group_heads * tok_rows
    zero_rows = jnp.zeros((total_rows,), jnp.float32)
    start_state = (jnp.full((total_rows,), MASKED, jnp.float32), zero_rows, zero_rows)
    running = start_state
    piece_keys = lax.all_gather(head_keys, "ctx", axis=0, tiled=True)
    piece_values = lax.all_gather(head_values, "ctx", axis=0, tiled=True)
    count_rows = piece_keys.shape[0]
    sub_rows = math.gcd(count_rows, tok_rows)
    piece_pos = piece_positions(block_order, count_rows, half_block)

    def sub_block(loop_state, block_parts):
        row_top, row_total, weighted = loop_state
        block_keys, block_values, block_pos = block_parts
        scores = (
            jnp.einsum("rd,kd->rk", query_rows, block_keys, preferred_element_type=jnp.float32)
            * score_scale
        )
        visible = block_pos[None, :] <= query_pos[:, None]
        scores = jnp.where(visible, scores, MASKED)
        new_top = jnp.maximum(row_top, jnp.max(scores, axis=1))
        rescale = jnp.exp(row_top - new_top)
        probability = jnp.where(visible, jnp.exp(scores - new_top[:, None]), 0.0)
        grad_prob = jnp.einsum(
            "rd,kd->rk", grad_rows, block_values, preferred_element_type=jnp.float32
        )
        row_total = row_total * rescale + jnp.sum(probability, axis=1)
        weighted = weighted * rescale + jnp.sum(probability * grad_prob, axis=1)
        return ((new_top, row_total, weighted), None)

    block_parts = (
        piece_keys.reshape(count_rows // sub_rows, sub_rows, HD),
        piece_values.reshape(count_rows // sub_rows, sub_rows, HD),
        piece_pos.reshape(count_rows // sub_rows, sub_rows),
    )
    running, _ = lax.scan(sub_block, running, block_parts)
    row_top, row_total, weighted = running
    log_total = row_top + jnp.log(row_total)
    delta_rows = weighted / row_total

    def visit_block(walk_keys, walk_values, owner_index):
        walk_pos = own_positions(block_order, owner_index, tok_rows)
        visible = walk_pos[None, :] <= query_pos[:, None]
        scores = (
            jnp.einsum("rd,kd->rk", query_rows, walk_keys, preferred_element_type=jnp.float32)
            * score_scale
        )
        probability = jnp.where(
            visible, jnp.exp(jnp.where(visible, scores, MASKED) - log_total[:, None]), 0.0
        )
        grad_prob = jnp.einsum(
            "rd,kd->rk", grad_rows, walk_values, preferred_element_type=jnp.float32
        )
        dscore = (probability * (grad_prob - delta_rows[:, None])).astype(jnp.bfloat16)
        prob_low = probability.astype(jnp.bfloat16)
        key_term = (
            jnp.einsum("rk,rd->kd", dscore, query_rows, preferred_element_type=jnp.float32)
            * score_scale
        )
        value_term = jnp.einsum(
            "rk,rd->kd", prob_low, grad_rows, preferred_element_type=jnp.float32
        )
        query_term = jnp.dot(dscore, walk_keys, preferred_element_type=jnp.float32) * score_scale
        return (key_term, value_term, query_term)

    zero_kv = jnp.zeros((tok_rows, HD), jnp.float32)
    zero_q = jnp.zeros((total_rows, HD), jnp.float32)

    def along_step(cycle_step, loop_state):
        walk_k, walk_v, sum_k, sum_v, acc_q = loop_state
        contrib = visit_block(walk_k, walk_v, (ctx_index - cycle_step) % cycle_size)
        walk_k, walk_v, sum_k, sum_v = (
            passed_along(walk_k.astype(jnp.float32), "ctx", 1).astype(walk_k.dtype),
            passed_along(walk_v.astype(jnp.float32), "ctx", 1).astype(walk_v.dtype),
            passed_along(sum_k + contrib[0], "ctx", 1),
            passed_along(sum_v + contrib[1], "ctx", 1),
        )
        return (walk_k, walk_v, sum_k, sum_v, acc_q + contrib[2])

    walk_k, walk_v, sum_k, sum_v, acc_q = lax.fori_loop(
        0, cycle_size - 1, along_step, (head_keys, head_values, zero_kv, zero_kv, zero_q)
    )
    contrib = visit_block(walk_k, walk_v, (ctx_index + 1) % cycle_size)
    grad_key, grad_value = passed_along((sum_k + contrib[0], sum_v + contrib[1]), "ctx", 1)
    acc_q = acc_q + contrib[2]
    grad_queries = (
        acc_q.reshape(group_heads, tok_rows, HD)
        .transpose(1, 0, 2)
        .reshape(tok_rows, group_heads * HD)
        .astype(jnp.bfloat16)
    )
    key_grad_pre = unrotate(grad_key, cosine_table, sine_table)
    all_key, all_value = (
        lax.all_gather(key_grad_pre, ("row", "col"), axis=1, tiled=True),
        lax.all_gather(grad_value, ("row", "col"), axis=1, tiled=True),
    )
    key_low = all_key.astype(jnp.bfloat16)
    value_low = all_value.astype(jnp.bfloat16)
    grad_inputs = (
        jnp.einsum("tk,dk->td", key_low, w_key, preferred_element_type=jnp.float32)
        + jnp.einsum("tk,dk->td", value_low, w_value, preferred_element_type=jnp.float32)
    ).astype(jnp.bfloat16)
    weight_key = jnp.einsum("td,tk->dk", inputs, key_low, preferred_element_type=jnp.float32)
    weight_value = jnp.einsum("td,tk->dk", inputs, value_low, preferred_element_type=jnp.float32)
    bias_key = jnp.sum(all_key, axis=0)
    bias_value = jnp.sum(all_value, axis=0)
    grad_w_key, grad_w_value, grad_key_bias, grad_value_bias = (
        lax.psum_scatter(weight_key, "ctx", scatter_dimension=1, tiled=True),
        lax.psum_scatter(weight_value, "ctx", scatter_dimension=1, tiled=True),
        lax.psum_scatter(bias_key, "ctx", scatter_dimension=0, tiled=True),
        lax.psum_scatter(bias_value, "ctx", scatter_dimension=0, tiled=True),
    )
    return (
        grad_inputs,
        grad_queries,
        grad_w_key.astype(jnp.bfloat16),
        grad_w_value.astype(jnp.bfloat16),
        grad_key_bias,
        grad_value_bias,
    )


def solution(mesh):
    return jax.shard_map(
        body,
        mesh=mesh,
        in_specs=(
            P("ctx", ("row", "col")),
            P("ctx", ("row", "col")),
            P("ctx", ("row", "col")),
            P(("row", "col"), None),
            P(("row", "col"), None),
            P(),
            P(),
        ),
        out_specs=(
            P("ctx", ("row", "col")),
            P("ctx", ("row", "col")),
            P(("row", "col"), "ctx"),
            P(("row", "col"), "ctx"),
            P("ctx"),
            P("ctx"),
        ),
        check_vma=False,
    )
```

profile of v0, /device:TPU:8, one launch (start us, length us, event | category | flops | bytes accessed | tf_op | source)
XLA Modules:
  0.0 1113.7 jit_solution(4720809597557330664)
XLA Ops:
  16.8 35.7 %reduce-scatter.5.cloned.1.call-done = f32[128,128]{1,0:T(8,128)} async-done(((f32[128,1024]{1,0:T(8,128)}), f32[128,128]{1,0:T(8,128)}) %reduce-scatter.5.cloned.1.call-update) | async-done | bytes 65552 | tf_op jit(solution)/shard_map/reduce_scatter | solution.py:83
  54.5 40.3 %reduce-scatter.7.cloned.1.call-done = f32[128,128]{1,0:T(8,128)} async-done(((f32[128,1024]{1,0:T(8,128)}), f32[128,128]{1,0:T(8,128)}) %reduce-scatter.7.cloned.1.call-update) | async-done | bytes 65552 | tf_op jit(solution)/shard_map/reduce_scatter | solution.py:84
  99.2 76.9 %all-gather.3.cloned.1.call-done = bf16[4096,128]{1,0:T(8,128)(2,1)} async-done(((bf16[128,128]{1,0:T(8,128)(2,1)}), bf16[4096,128]{1,0:T(8,128)(2,1)}) %all-gather.3.cloned.1.call-update) | async-done | bytes 1048592 | tf_op jit(solution)/shard_map/all_gather | solution.py:104
  176.1 77.1 %all-gather.5.cloned.1.call-done = bf16[4096,128]{1,0:T(8,128)(2,1)} async-done(((bf16[128,128]{1,0:T(8,128)(2,1)}), bf16[4096,128]{1,0:T(8,128)(2,1)}) %all-gather.5.cloned.1.call-update) | async-done | bytes 1048592 | tf_op jit(solution)/shard_map/all_gather | solution.py:105
  253.1 72.4 %while.40 = (s32[]{:T(128)}, f32[1024]{0:T(1024)S(1)}, f32[1024]{0:T(1024)S(1)}, f32[1024]{0:T(1024)S(1)}, s32[32,128]{1,0:T(8,128)S(1)}, /*index=5*/bf16[32,128...) while((s32[]{:T(128)}, f32[1024]{0:T(1024)S(1)}, ...), condition=%wide.region_7.8_spmd.clone, body=%wide.region_3.7_spmd.clone.sunk | while | flops 68819968 | bytes 2256020 | solution.py:134
  326.8 483.5 %while.41 = (s32[]{:T(128)}, bf16[128,128]{1,0:T(8,128)(2,1)}, bf16[128,128]{1,0:T(8,128)(2,1)}, f32[128,128]{1,0:T(8,128)}, f32[128,128]{1,0:T(8,128)S(1)}, /*i...) while((s32[]{:T(128)}, bf16[128,128]{1,0:T(8,128)(2,1)}, ...), condition=%wide.region_9.10_spmd.clone, body=%wide.region_8.9_spmd.clone.sunk | while | flops 169395472 | bytes 5752874 | solution.py:178
  352.0 6.2 collective-permute-done.2
  367.5 6.2 collective-permute-done.2
  383.1 6.2 collective-permute-done.2
  398.7 6.2 collective-permute-done.2
  414.2 6.2 collective-permute-done.2
  429.8 6.2 collective-permute-done.2
  445.4 6.2 collective-permute-done.2
  460.9 6.2 collective-permute-done.2
  507.6 6.2 collective-permute-done.2
  647.7 6.2 collective-permute-done.2
  725.6 6.2 collective-permute-done.2
  803.4 6.2 collective-permute-done.2
  812.3 6.8 collective-permute-done.5
  819.1 27.9 %all_gather.15 = f32[128,1024]{1,0:T(8,128)S(1)} all-gather(f32[128,128]{1,0:T(8,128)S(1)} %collective-permute-done.5), channel_id=1, replica_groups=mesh['ctx'=32,'row'=4,'col'=2] {'row','col'}, dimensions={1}, use_global_device_ids=true | all-gather | bytes 589824 | tf_op jit(solution)/shard_map/all_gather | solution.py:193
  853.1 7.3 collective-permute-done.4
  860.9 30.1 %all_gather.14 = f32[128,1024]{1,0:T(8,128)S(1)} all-gather(f32[128,128]{1,0:T(8,128)S(1)} %pad_maximum_fusion), channel_id=1, replica_groups=mesh['ctx'=32,'row'=4,'col'=2] {'row','col'}, dimensions={1}, use_global_device_ids=true | all-gather | bytes 589824 | tf_op jit(solution)/shard_map/all_gather | solution.py:192
  899.5 66.5 %all-reduce.2 = (f32[1024]{0:T(1024)S(1)}, f32[1024]{0:T(1024)S(1)}) all-reduce(f32[1024]{0:T(1024)S(1)} %reduce_sum.46, f32[1024]{0:T(1024)S(1)} %reduce_sum.47), channel_id=6, replica_groups=mesh['ctx'=32,'row'=4,'col'=2] {'ctx'}, use_global_device_ids=true, to_apply=%region_13.14.clone | all-reduce | flops 2048 | bytes 16384
  976.3 128.9 %reduce-scatter.9.cloned.1.call-done = f32[1024,32]{0,1:T(8,128)} async-done(((f32[1024,1024]{0,1:T(8,128)}), f32[1024,32]{0,1:T(8,128)}) %reduce-scatter.9.cloned.1.call-update) | async-done | bytes 131088 | tf_op jit(solution)/shard_map/reduce_scatter | solution.py:206
  (924 shorter events, 523.1 us)
Async XLA Ops:
  7.2 45.4 %reduce-scatter.5.cloned.1.call-start = ((), (), s32[]{:S(2)}) async-start(), calls=%async_computation.4 | async-start | bytes 589824 | tf_op jit(solution)/shard_map/reduce_scatter | solution.py:83
  11.0 83.8 %reduce-scatter.7.cloned.1.call-start = ((), (), s32[]{:S(2)}) async-start(), calls=%async_computation.5 | async-start | bytes 589824 | tf_op jit(solution)/shard_map/reduce_scatter | solution.py:84
  14.0 162.1 %all-gather.3.cloned.1.call-start = ((), (), s32[]{:S(2)}) async-start(), calls=%async_computation.6 | async-start | bytes 1081344 | tf_op jit(solution)/shard_map/all_gather | solution.py:104
  54.5 198.7 %all-gather.5.cloned.1.call-start = ((), (), s32[]{:S(2)}) async-start(), calls=%async_computation.7 | async-start | bytes 1081344 | tf_op jit(solution)/shard_map/all_gather | solution.py:105
  96.3 878.5 %reduce-scatter.11.cloned.1.call-start = ((), (), s32[]{:S(2)}) async-start(), calls=%async_computation.9 | async-start | bytes 4325376 | tf_op jit(solution)/shard_map/reduce_scatter | solution.py:207
  327.6 10.3 collective-permute-start.1
  328.6 9.3 collective-permute-start
  334.7 7.6 collective-permute-start.2
  350.5 7.6 collective-permute-start.2
  366.1 7.6 collective-permute-start.2
  381.7 7.6 collective-permute-start.2
  397.2 7.6 collective-permute-start.2
  412.8 7.6 collective-permute-start.2
  428.4 7.6 collective-permute-start.2
  443.9 7.6 collective-permute-start.2
  490.6 7.6 collective-permute-start.2
  506.2 7.6 collective-permute-start.2
  568.5 7.6 collective-permute-start.2
  646.3 7.6 collective-permute-start.2
  708.6 7.6 collective-permute-start.2
  724.1 7.6 collective-permute-start.2
  786.4 7.6 collective-permute-start.2
  802.0 7.6 collective-permute-start.2
  850.6 254.7 %reduce-scatter.9.cloned.1.call-start = ((), (), s32[]{:S(2)}) async-start(), calls=%async_computation.8 | async-start | bytes 4325376 | tf_op jit(solution)/shard_map/reduce_scatter | solution.py:206
  (124 other events, 1136.2 us)
Sparse Core Ops, SparseCore 0:
  11.1 41.4 reduce-scatter.4
  55.2 39.4 reduce-scatter.6
  97.6 78.4 all-gather.2
  178.7 74.3 all-gather.4
  850.7 124.0 reduce-scatter.10
  979.5 125.7 reduce-scatter.8
where the time goes:
time: 1130 us; the launch traced here: 1110 us
  waiting for transfers between devices  600 us (53%)
  matrix products  232 us (21%)
  blocking collectives  124 us (11%)
  local copies, waits for them, and re-layouts  77.7 us (7%)
  other arithmetic  57.1 us (5%)
  between operations  15.1 us (1%)
    ppermute x126, waiting for transfers between devices, passed_along(): return lax.ppermute(block, axis, route)  236 us
    reduce_scatter x1, waiting for transfers between devices, body(): lax.psum_scatter(weight_key, 'ctx', scatter_dimension=1, tiled=True)  129 us
    all_gather x1, waiting for transfers between devices, body(): piece_values = lax.all_gather(head_values, 'ctx', axis=0, tiled=True)  77.1 us
    all_gather x1, waiting for transfers between devices, body(): piece_keys = lax.all_gather(head_keys, 'ctx', axis=0, tiled=True)  76.9 us
    unnamed x1, blocking collectives  66.5 us
    dot_general x32, matrix products, visit_block(): jnp.einsum('rk,rd->kd', dscore, query_rows, preferred_element_type=jnp.fl...  55.2 us
    dot_general x32, matrix products, visit_block(): jnp.einsum('rd,kd->rk', query_rows, walk_keys, preferred_element_type=jnp...  52 us
    while x94, local copies, waits for them, and re-layouts  47.1 us
  transfers between devices with their start and end apart: 132, of which 100 were waited for; matrix products, arithmetic and copies ran while one was open for 23% of the time, Pallas kernels for 0%

commit v1 on v0

v1 whole, which is shorter than its diff:
```python
import functools
import math

import jax
import jax.numpy as jnp
import numpy as np
from jax import lax
from jax.experimental import pallas as pl
from jax.experimental.pallas import tpu as pltpu
from jax.sharding import PartitionSpec as P

HD = 128
ROPE_BASE = 1000000.0
MASKED = -1e30
F32 = jnp.float32
BF16 = jnp.bfloat16
SCALE = HD ** -0.5
LOG2E = math.log2(math.e)
MESH = pl.DeviceIdType.MESH
VMEM = pltpu.VMEM

NCTX = 32
NZ = 8
NROW = 4
NCOL = 2
NHEAD = 8
TOK = 128
BLK = 64
TILE = 256
SEQ = NCTX * TOK
ROWS = 8 * BLK
MODEL = 1024
HEAD_STEPS = ((2, 1), (2, 0), (1, 1), (3, 1), (1, 0), (3, 0), (0, 1))


class Place:
    def __init__(self):
        self.ctx = lax.axis_index("ctx")
        self.row = lax.axis_index("row")
        self.col = lax.axis_index("col")
        self.core = lax.rem(self.ctx, 2)
        self.z = lax.rem(lax.div(self.ctx, 2), NZ)
        self.xh = lax.div(self.ctx, 2 * NZ)
        self.head = self.row * NCOL + self.col

    def slot(self, xh, z, core):
        return (xh * NZ + lax.rem(z + 2 * NZ, NZ)) * 2 + core

    def ctx_device(self, xh, z, core):
        return (self.slot(xh, z, core), self.row, self.col)

    def right(self):
        return self.ctx_device(self.xh, self.z + 1, self.core)

    def left(self):
        return self.ctx_device(self.xh, self.z - 1, self.core)

    def across(self):
        return self.ctx_device(1 - self.xh, self.z, self.core)

    def sibling(self):
        return self.ctx_device(self.xh, self.z, 1 - self.core)

    def head_peer(self, step):
        row = lax.rem(self.row + step[0], NROW)
        col = lax.rem(self.col + step[1], NCOL)
        return row, col

    def head_device(self, step):
        row, col = self.head_peer(step)
        return (self.ctx, row, col)

    def head_source(self, step):
        row = lax.rem(self.row + NROW - step[0], NROW)
        col = lax.rem(self.col + NCOL - step[1], NCOL)
        return row * NCOL + col

    def greet(self):
        barrier = pltpu.get_barrier_semaphore()
        others = [self.right(), self.left(), self.across(), self.sibling()]
        others += [self.head_device(step) for step in HEAD_STEPS]
        for device in others:
            pl.semaphore_signal(barrier, inc=1, device_id=device, device_id_type=MESH)
        pl.semaphore_wait(barrier, len(others))


def remote(src, dst, send_sem, recv_sem, device):
    return pltpu.make_async_remote_copy(
        src_ref=src,
        dst_ref=dst,
        send_sem=send_sem,
        recv_sem=recv_sem,
        device_id=device,
        device_id_type=MESH,
    )


def turned(tensor):
    return jnp.concatenate([tensor[:, HD // 2 :], tensor[:, : HD // 2]], axis=1)


def gather_kernel(
    x_ref, wk_ref, wv_ref, bias_ref, cos_ref, sin_ref, kv_ref,
    part_k, part_v, got_k, got_v, ks, kr, vs, vr, ring_send, ring_recv,
):
    me = Place()
    me.greet()
    x = x_ref[...]
    sends = []

    def partial(head):
        columns = pl.ds(pl.multiple_of(head * HD, HD), HD)
        return (
            jnp.dot(x, wk_ref[:, columns], preferred_element_type=F32),
            jnp.dot(x, wv_ref[:, columns], preferred_element_type=F32),
        )

    for i, step in enumerate(HEAD_STEPS):
        row, col = me.head_peer(step)
        key, value = partial(row * NCOL + col)
        part_k[i] = key.astype(part_k.dtype)
        part_v[i] = value.astype(part_v.dtype)
        device = (me.ctx, row, col)
        for part, got, ss, rs in ((part_k, got_k, ks, kr), (part_v, got_v, vs, vr)):
            copy = remote(part.at[i], got.at[i], ss.at[i], rs.at[i], device)
            copy.start()
            sends.append(copy)
    key, value = partial(me.head)
    key = key + bias_ref[pl.ds(me.head, 1), :]
    for i in range(len(HEAD_STEPS)):
        sends[2 * i].wait_recv()
        key = key + got_k[i].astype(F32)
        sends[2 * i + 1].wait_recv()
        value = value + got_v[i].astype(F32)
    own = me.slot(me.xh, me.z, me.core)
    kv_ref[own, 0] = (key * cos_ref[...] + turned(key) * sin_ref[...]).astype(BF16)
    kv_ref[own, 1] = value.astype(BF16)

    targets = (me.right(), me.left(), me.across(), me.sibling())

    def pass_on(slot, directions):
        for way in directions:
            copy = remote(
                kv_ref.at[slot], kv_ref.at[slot], ring_send.at[way, slot], ring_recv.at[slot], targets[way]
            )
            copy.start()
            sends.append(copy)

    def arrived(slot):
        remote(
            kv_ref.at[slot], kv_ref.at[slot], ring_send.at[0, slot], ring_recv.at[slot], targets[3]
        ).wait_recv()

    R, L, X, C = range(4)
    pass_on(own, (R, L, X, C))
    here, there = me.xh, 1 - me.xh
    plan = (
        (here, -1, (R, C)), (here, 1, (L, C)),
        (there, 0, (R, L, C)),
        (here, -2, (R, C)), (here, 2, (L, C)),
        (there, -1, (R, C)), (there, 1, (L, C)),
        (here, -3, (R, C)), (here, 3, (C,)),
        (there, -2, (R, C)), (there, 2, (L, C)),
        (here, -4, (C,)),
        (there, -3, (C,)), (there, 3, (L, C)),
        (there, 4, (C,)),
    )
    for xh, dz, ways in plan:
        slot = me.slot(xh, me.z + dz, me.core)
        arrived(slot)
        pass_on(slot, ways)
    arrived(me.slot(here, me.z, 1 - me.core))
    for xh, dz, _ in plan:
        arrived(me.slot(xh, me.z + dz, 1 - me.core))
    for copy in sends:
        copy.wait_send()


def gather_keys(x, w_key, w_value, bias, cos, sin):
    steps = len(HEAD_STEPS)
    vmem = pl.BlockSpec(memory_space=VMEM)
    dma = pltpu.SemaphoreType.DMA
    return pl.pallas_call(
        gather_kernel,
        name="project_gather",
        out_shape=jax.ShapeDtypeStruct((NCTX, 2, TOK, HD), BF16),
        in_specs=[vmem] * 6,
        out_specs=vmem,
        scratch_shapes=[
            VMEM((steps, TOK, HD), F32),
            VMEM((steps, TOK, HD), BF16),
            VMEM((steps, TOK, HD), F32),
            VMEM((steps, TOK, HD), BF16),
            dma((steps,)), dma((steps,)), dma((steps,)), dma((steps,)),
            dma((4, NCTX)), dma((NCTX,)),
        ],
        compiler_params=pltpu.CompilerParams(
            collective_id=0, has_side_effects=True, vmem_limit_bytes=40 * 2**20
        ),
    )(x, w_key, w_value, bias, cos, sin)


def attend_kernel(
    order_ref, q_ref, g_ref, kv_ref, dq_ref, dkv_ref,
    keys, values, rows_q, rows_g, cols_q, cols_g, sum_k, sum_v, sum_q,
):
    ctx = lax.axis_index("ctx")
    first, second = order_ref[2 * ctx], order_ref[2 * ctx + 1]
    low_half = jnp.where(first < second, 0, 1)
    low_block = jnp.minimum(first, second)
    high_block = jnp.maximum(first, second)

    def collect(i, carry):
        for half in range(2):
            block = order_ref[2 * i + half]
            to = pl.ds(pl.multiple_of(block * BLK, BLK), BLK)
            keys[to, :] = kv_ref[i, 0, half * BLK : (half + 1) * BLK, :]
            values[to, :] = kv_ref[i, 1, half * BLK : (half + 1) * BLK, :]
        return carry

    lax.fori_loop(0, NCTX, collect, 0)
    for half in range(2):
        index = jnp.where(low_half == half, 1, 0)
        for head in range(8):
            place = (slice(half * BLK, (half + 1) * BLK), slice(head * HD, (head + 1) * HD))
            rows_q[index, head * BLK : (head + 1) * BLK, :] = q_ref[place]
            rows_g[index, head * BLK : (head + 1) * BLK, :] = g_ref[place]
    for index in range(2):
        cols_q[index] = rows_q[index].T
        cols_g[index] = rows_g[index].T

    step = (
        lax.broadcasted_iota(jnp.int32, (TILE, ROWS), 0)
        - lax.broadcasted_iota(jnp.int32, (TILE, ROWS), 1) % BLK
    )
    blocks = (high_block, low_block)

    def tile_scores(index, tile, masked):
        here = pl.ds(pl.multiple_of(tile * TILE, TILE), TILE)
        key, value = keys[here, :], values[here, :]
        score = jnp.dot(key, cols_q[index], preferred_element_type=F32) * (SCALE * LOG2E)
        grad = jnp.dot(value, cols_g[index], preferred_element_type=F32)
        if masked:
            visible = step <= blocks[index] * BLK - tile * TILE
            score = jnp.where(visible, score, MASKED)
        return here, key, score, grad

    for index in range(2):
        last = blocks[index] // (TILE // BLK)

        def totals(tile, state, masked=False):
            top, total, weighted = state
            _, _, score, grad = tile_scores(index, tile, masked)
            new_top = jnp.maximum(top, jnp.max(score, axis=0, keepdims=True))
            prob = jnp.exp2(score - new_top)
            rescale = jnp.exp2(top - new_top)
            total = total * rescale + jnp.sum(prob, axis=0, keepdims=True)
            weighted = weighted * rescale + jnp.sum(prob * grad, axis=0, keepdims=True)
            return new_top, total, weighted

        zero = jnp.zeros((1, ROWS), F32)
        state = (jnp.full((1, ROWS), MASKED, F32), zero, zero)
        state = lax.fori_loop(0, last, totals, state)
        top, total, weighted = totals(last, state, masked=True)
        log_total = top + jnp.log2(total)
        delta = weighted / total
        sum_q[...] = jnp.zeros_like(sum_q)

        def gradients(tile, masked=False):
            here, key, score, grad = tile_scores(index, tile, masked)
            prob = jnp.exp2(score - log_total)
            dscore = (prob * (grad - delta)).astype(BF16)
            prob_low = prob.astype(BF16)
            key_term = jnp.dot(dscore, rows_q[index], preferred_element_type=F32)
            value_term = jnp.dot(prob_low, rows_g[index], preferred_element_type=F32)
            if index == 0:
                sum_k[here, :] = key_term
                sum_v[here, :] = value_term
            else:
                sum_k[here, :] += key_term
                sum_v[here, :] += value_term
            sum_q[...] += jnp.dot(key.T, dscore, preferred_element_type=F32)

        @pl.loop(0, last)
        def _(tile):
            gradients(tile)

        gradients(last, masked=True)
        if index == 0:

            @pl.loop(last + 1, SEQ // TILE)
            def _(tile):
                here = pl.ds(pl.multiple_of(tile * TILE, TILE), TILE)
                sum_k[here, :] = jnp.zeros((TILE, HD), F32)
                sum_v[here, :] = jnp.zeros((TILE, HD), F32)

        query = (sum_q[...] * SCALE).T.astype(BF16)
        half = low_half if index == 1 else 1 - low_half
        to = pl.ds(pl.multiple_of(half * BLK, BLK), BLK)
        for head in range(8):
            dq_ref[to, head * HD : (head + 1) * HD] = query[head * BLK : (head + 1) * BLK, :]

    def spread(i, carry):
        core, z, xh = lax.rem(i, 2), lax.rem(lax.div(i, 2), NZ), lax.div(i, 2 * NZ)
        for half in range(2):
            block = order_ref[2 * i + half]
            src = pl.ds(pl.multiple_of(block * BLK, BLK), BLK)
            rows = slice(half * BLK, (half + 1) * BLK)
            dkv_ref[core, z, xh, 0, rows, :] = (sum_k[src, :] * SCALE).astype(BF16)
            dkv_ref[core, z, xh, 1, rows, :] = sum_v[src, :].astype(BF16)
        return carry

    lax.fori_loop(0, NCTX, spread, 0)


def attend(order, queries, out_grad, kv):
    vmem = pl.BlockSpec(memory_space=VMEM)
    return pl.pallas_call(
        attend_kernel,
        name="attend",
        out_shape=(
            jax.ShapeDtypeStruct((TOK, MODEL), BF16),
            jax.ShapeDtypeStruct((2, NZ, 2, 2, TOK, HD), BF16),
        ),
        in_specs=[pl.BlockSpec(memory_space=pltpu.SMEM), vmem, vmem, vmem],
        out_specs=(vmem, vmem),
        scratch_shapes=[
            VMEM((SEQ, HD), BF16), VMEM((SEQ, HD), BF16),
            VMEM((2, ROWS, HD), BF16), VMEM((2, ROWS, HD), BF16),
            VMEM((2, HD, ROWS), BF16), VMEM((2, HD, ROWS), BF16),
            VMEM((SEQ, HD), F32), VMEM((SEQ, HD), F32),
            VMEM((HD, ROWS), F32),
        ],
        compiler_params=pltpu.CompilerParams(vmem_limit_bytes=40 * 2**20),
    )(order, queries, out_grad, kv)


RIGHT_FROM = (4, 3)
LEFT_FROM = (3, 4)
ORDER = (4, 3, 5, 2, 6, 1, 7, 0)


class Ring:
    def __init__(self, me, send, recv, cross, send_sem, recv_sem, cross_send, cross_recv, mine):
        self.me, self.send, self.recv, self.cross = me, send, recv, cross
        self.send_sem, self.recv_sem = send_sem, recv_sem
        self.cross_send, self.cross_recv = cross_send, cross_recv
        self.mine = mine
        self.copies = {}

    def sends(self, p, way, distance):
        i = p * 7 + (distance - 1 if way == 0 else RIGHT_FROM[p] + distance - 1)
        begin = (RIGHT_FROM if way == 0 else LEFT_FROM)[p]
        term = self.mine(p, distance if way == 0 else NZ - distance)
        if distance < begin:
            term = term + self.take(p, way, distance + 1)
        self.send[i] = term.astype(self.send.dtype)
        device = self.me.right() if way == 0 else self.me.left()
        copy = remote(
            self.send.at[i], self.recv.at[i], self.send_sem.at[i], self.recv_sem.at[i], device
        )
        copy.start()
        self.copies[p, way, distance] = copy, i

    def take(self, p, way, distance):
        copy, i = self.copies[p, way, distance]
        copy.wait_recv()
        return self.recv[i].astype(F32)

    def finish_other(self):
        term = self.mine(1, 0) + self.take(1, 0, 1) + self.take(1, 1, 1)
        self.cross[0] = term.astype(self.cross.dtype)
        self.cross_copy = remote(
            self.cross.at[0], self.cross.at[1], self.cross_send, self.cross_recv, self.me.across()
        )
        self.cross_copy.start()

    def finish_own(self):
        term = self.mine(0, 0) + self.take(0, 0, 1) + self.take(0, 1, 1)
        self.cross_copy.wait_recv()
        return term + self.cross[1].astype(F32)

    def drain(self):
        for copy, _ in self.copies.values():
            copy.wait_send()
        self.cross_copy.wait_send()


RING_ROUNDS = (
    ((0, 0, 4), (1, 1, 4)),
    ((1, 0, 3), (0, 1, 3)),
    ((0, 0, 3), (1, 1, 3)),
    ((1, 0, 2), (0, 1, 2)),
    ((0, 0, 2), (1, 1, 2)),
    ((1, 0, 1), (0, 1, 1)),
    ((1, 1, 1), (0, 0, 1)),
)


def finish_kernel(
    x_ref, wk_hbm, wv_hbm, cos_ref, sin_ref, dkv_ref,
    gx_ref, gw_ref, gb_ref,
    wk, wv, both_x, pair, low, low_pair, bias, bias_pair, terms,
    send_a, recv_a, cross_a, send_b, recv_b, cross_b, send_c, recv_c, cross_c,
    w_sem, x_sem, pair_send, pair_recv, low_send, low_recv, bias_send, bias_recv,
    fwd_send, fwd_recv, sems_a, sems_b, sems_c, cross_sems,
):
    me = Place()
    load_k = pltpu.make_async_copy(wk_hbm, wk, w_sem.at[0])
    load_v = pltpu.make_async_copy(wv_hbm, wv, w_sem.at[1])
    load_k.start()
    load_v.start()
    me.greet()
    sibling = me.sibling()
    core, other = me.core, 1 - me.core

    def along(dz):
        return lax.rem(me.z + dz, NZ)

    pair_copies = {}
    for dz in ORDER:
        z = along(dz)
        copy = remote(dkv_ref.at[other, z], pair.at[z], pair_send.at[z], pair_recv.at[z], sibling)
        copy.start()
        pair_copies[dz] = copy
    share_x = remote(x_ref, both_x.at[1], x_sem.at[0], x_sem.at[1], sibling)
    share_x.start()
    both_x[0] = x_ref[...]
    seen = set()

    def side(p):
        return me.xh if p == 0 else 1 - me.xh

    def mine_a(p, dz):
        if dz not in seen:
            pair_copies[dz].wait_recv()
            seen.add(dz)
        z = along(dz)
        return dkv_ref[core, z, side(p)].astype(F32) + pair[z, side(p)].astype(F32)

    ring = Ring(
        me, send_a, recv_a, cross_a, sems_a.at[0], sems_a.at[1], cross_sems.at[0], cross_sems.at[1], mine_a
    )
    for group in RING_ROUNDS:
        for item in group:
            ring.sends(*item)
    ring.finish_other()
    total = ring.finish_own()
    key, value = total[0], total[1]
    key = key * cos_ref[...] - turned(key) * sin_ref[...]
    low[me.head, 0] = key.T.astype(BF16)
    low[me.head, 1] = value.T.astype(BF16)
    key_sum = jnp.sum(key, axis=0, keepdims=True)
    value_sum = jnp.sum(value, axis=0, keepdims=True)
    line = lax.broadcasted_iota(jnp.int32, (8, HD), 0)
    bias[me.head] = jnp.where(line == 0, key_sum, jnp.where(line == 1, value_sum, 0.0))

    copies = []
    for i, step in enumerate(HEAD_STEPS):
        device = me.head_device(step)
        for array, ss, rs in ((low, low_send, low_recv), (bias, bias_send, bias_recv)):
            copy = remote(array.at[me.head], array.at[me.head], ss.at[i], rs.at[i], device)
            copy.start()
            copies.append(copy)

    forwards = []

    def forward(head, i):
        copy = remote(low.at[head], low_pair.at[head], fwd_send.at[i], fwd_recv.at[i], sibling)
        copy.start()
        forwards.append(copy)

    forward(me.head, 7)
    for i in (6, 4, 5, 2, 3, 1, 0):
        source = me.head_source(HEAD_STEPS[i])
        remote(low.at[source], low.at[source], low_send.at[i], low_recv.at[i], sibling).wait_recv()
        forward(source, i)
    for i in range(7):
        copies[2 * i + 1].wait_recv()
    share_bias = remote(bias, bias_pair, x_sem.at[2], x_sem.at[3], sibling)
    share_bias.start()
    share_x.wait_recv()
    for copy in forwards:
        copy.wait_recv()

    tokens = both_x[...].reshape(2 * TOK, MODEL)

    def chip_rows(z, xh):
        chip = xh * NZ + z
        head, half = lax.div(chip, 2), lax.rem(chip, 2)
        rows = pl.ds(pl.multiple_of(half * 64 + core * 32, 32), 32)
        return jnp.concatenate(
            [
                jnp.concatenate([low[head, part, rows, :], low_pair[head, part, rows, :]], axis=1)
                for part in range(2)
            ],
            axis=0,
        )

    def weigh(dz):
        z = along(dz)
        left = jnp.concatenate([chip_rows(z, side(0)), chip_rows(z, side(1))], axis=0)
        out = jnp.dot(left, tokens, preferred_element_type=F32)
        terms[dz] = out.reshape(2, 64, MODEL)

    def mine_b(p, dz):
        return terms[dz, p]

    def mine_c(p, dz):
        head = lax.div(side(p) * NZ + along(dz), 2)
        return bias[head] + bias_pair[head]

    ring_b = Ring(
        me, send_b, recv_b, cross_b, sems_b.at[0], sems_b.at[1], cross_sems.at[2], cross_sems.at[3], mine_b
    )
    ring_c = Ring(
        me, send_c, recv_c, cross_c, sems_c.at[0], sems_c.at[1], cross_sems.at[4], cross_sems.at[5], mine_c
    )

    def both(group):
        for item in group:
            ring_b.sends(*item)
        for item in group:
            ring_c.sends(*item)

    weigh(4)
    for item in RING_ROUNDS[0]:
        ring_b.sends(*item)
    weigh(3)
    weigh(5)
    for item in RING_ROUNDS[1]:
        ring_b.sends(*item)
    share_bias.wait_recv()
    for group in RING_ROUNDS[:2]:
        for item in group:
            ring_c.sends(*item)
    for dz in (2, 6, 1, 7, 0):
        weigh(dz)
    both(RING_ROUNDS[2])
    load_k.wait()
    load_v.wait()
    low_key = low[:, 0].reshape(NHEAD * HD, TOK)
    low_value = low[:, 1].reshape(NHEAD * HD, TOK)
    gx = jnp.dot(wk[...], low_key, preferred_element_type=F32)
    gx = gx + jnp.dot(wv[...], low_value, preferred_element_type=F32)
    gx_ref[...] = gx.T.astype(BF16)
    for group in RING_ROUNDS[3:]:
        both(group)
    ring_b.finish_other()
    ring_c.finish_other()
    gw_ref[...] = ring_b.finish_own().astype(BF16)
    gb_ref[...] = ring_c.finish_own()

    for copy in pair_copies.values():
        copy.wait_send()
    share_x.wait_send()
    share_bias.wait_send()
    for copy in copies + forwards:
        copy.wait_send()
    ring.drain()
    ring_b.drain()
    ring_c.drain()


def finish(x, w_key, w_value, cos, sin, dkv):
    vmem = pl.BlockSpec(memory_space=VMEM)
    hbm = pl.BlockSpec(memory_space=pl.ANY)
    dma = pltpu.SemaphoreType.DMA
    return pl.pallas_call(
        finish_kernel,
        name="finish",
        out_shape=(
            jax.ShapeDtypeStruct((TOK, MODEL), BF16),
            jax.ShapeDtypeStruct((64, MODEL), BF16),
            jax.ShapeDtypeStruct((8, HD), F32),
        ),
        in_specs=[vmem, hbm, hbm, vmem, vmem, vmem],
        out_specs=(vmem, vmem, vmem),
        scratch_shapes=[
            VMEM((MODEL, NHEAD * HD), BF16), VMEM((MODEL, NHEAD * HD), BF16),
            VMEM((2, TOK, MODEL), BF16),
            VMEM((NZ, 2, 2, TOK, HD), BF16),
            VMEM((NHEAD, 2, HD, TOK), BF16), VMEM((NHEAD, 2, HD, TOK), BF16),
            VMEM((NHEAD, 8, HD), F32), VMEM((NHEAD, 8, HD), F32),
            VMEM((NZ, 2, 64, MODEL), F32),
            VMEM((14, 2, TOK, HD), BF16), VMEM((14, 2, TOK, HD), BF16), VMEM((2, 2, TOK, HD), BF16),
            VMEM((14, 64, MODEL), BF16), VMEM((14, 64, MODEL), BF16), VMEM((2, 64, MODEL), BF16),
            VMEM((14, 8, HD), F32), VMEM((14, 8, HD), F32), VMEM((2, 8, HD), F32),
            dma((2,)), dma((4,)), dma((NZ,)), dma((NZ,)),
            dma((7,)), dma((7,)), dma((7,)), dma((7,)),
            dma((8,)), dma((8,)),
            dma((2, 14)), dma((2, 14)), dma((2, 14)), dma((6,)),
        ],
        compiler_params=pltpu.CompilerParams(
            collective_id=1, has_side_effects=True, vmem_limit_bytes=50 * 2**20
        ),
    )(x, w_key, w_value, cos, sin, dkv)


def rope_tables(order):
    frequency = (ROPE_BASE ** (-np.arange(HD // 2) * 2.0 / HD)).astype(np.float32)
    pair = lax.dynamic_slice_in_dim(order, 2 * lax.axis_index("ctx"), 2)
    positions = (pair[:, None] * BLK + jnp.arange(BLK, dtype=jnp.int32)[None, :]).reshape(TOK)
    angles = positions.astype(F32)[:, None] * jnp.asarray(frequency)[None, :]
    cos, sin = jnp.cos(angles), jnp.sin(angles)
    return jnp.concatenate([cos, cos], axis=1), jnp.concatenate([-sin, sin], axis=1)


def body(inputs, queries, out_grad, w_key, w_value, key_bias, block_order):
    cos, sin = rope_tables(block_order)
    kv = gather_keys(inputs, w_key, w_value, key_bias.reshape(NHEAD, HD), cos, sin)
    grad_queries, dkv = attend(block_order, queries, out_grad, kv)
    grad_inputs, grad_w, grad_b = finish(inputs, w_key, w_value, cos, sin, dkv)
    start = lax.rem(lax.axis_index("ctx"), 4) * 32
    grad_b = lax.dynamic_slice(grad_b, (0, start), (2, 32))
    return grad_inputs, grad_queries, grad_w[:32].T, grad_w[32:].T, grad_b[0], grad_b[1]


def solution(mesh):
    return jax.shard_map(
        body,
        mesh=mesh,
        in_specs=(
            P("ctx", ("row", "col")),
            P("ctx", ("row", "col")),
            P("ctx", ("row", "col")),
            P(("row", "col"), None),
            P(("row", "col"), None),
            P(),
            P(),
        ),
        out_specs=(
            P("ctx", ("row", "col")),
            P("ctx", ("row", "col")),
            P(("row", "col"), "ctx"),
            P(("row", "col"), "ctx"),
            P("ctx"),
            P("ctx"),
        ),
        check_vma=False,
    )
```

time: 1130 us -> 134 us (0.12); the launches traced: 1110 us -> 132 us
  waiting for transfers between devices: 600 us -> 0 us
  matrix products: 232 us -> 0 us
  blocking collectives: 124 us -> 0 us
  Pallas kernels: 0 us -> 121 us
  local copies, waits for them, and re-layouts: 77.7 us -> 8.21 us
  other arithmetic: 57.1 us -> 1.87 us
  between operations: 15.1 us -> 0.73 us
    ppermute x126 -> x0, waiting for transfers between devices: 236 us -> none  [passed_along(): return lax.ppermute(block, axis, route)]
    dot_general x230 -> x0, matrix products: 232 us -> none  [the longest x32 55.2 us: visit_block(): jnp.einsum('rk,rd->kd', dscore, query_rows, preferred_element_type=jnp.fl...]
    reduce_scatter x4 -> x0, waiting for transfers between devices: 209 us -> none  [the longest x1 129 us: body(): lax.psum_scatter(weight_key, 'ctx', scatter_dimension=1, tiled=True)]
    all_gather x2 -> x0, waiting for transfers between devices: 154 us -> none  [the longest x1 77.1 us: body(): piece_values = lax.all_gather(head_values, 'ctx', axis=0, tiled=True)]
    pallas_call x0 -> x3, Pallas kernels: none -> 121 us  [the longest x1 62.7 us: finish(): pl.pallas_call(finish_kernel, name='finish', out_shape=(jax.ShapeDtypeStr...]
    unnamed x1 -> x0, blocking collectives: 66.5 us -> none
    all_gather x2 -> x0, blocking collectives: 58 us -> none  [the longest x1 30.1 us: body(): lax.all_gather(key_grad_pre, ('row', 'col'), axis=1, tiled=True)]
    while x94 -> x0, local copies, waits for them, and re-layouts: 47.1 us -> none
  transfers between devices with their start and end apart: 132 -> 0, of which waited for: 100 -> 0; matrix products, arithmetic and copies ran while one was open for 23% -> 0% of each run, Pallas kernels for 0% -> 0%
where the time goes in v1:
time: 134 us; the launch traced here: 132 us
  Pallas kernels  121 us (90%)
  local copies, waits for them, and re-layouts  8.21 us (6%)
  other arithmetic  1.87 us (1%)
    pallas_call x1, Pallas kernels, finish(): pl.pallas_call(finish_kernel, name='finish', out_shape=(jax.ShapeDtypeStr...  62.7 us
    pallas_call x1, Pallas kernels, gather_keys(): pl.pallas_call(gather_kernel, name='project_gather', out_shape=jax.ShapeD...  40.7 us
    pallas_call x1, Pallas kernels, attend(): pl.pallas_call(attend_kernel, name='attend', out_shape=(jax.ShapeDtypeStr...  17.6 us
    unnamed x21, local copies, waits for them, and re-layouts  6.87 us

profile of v1, /device:TPU:8, one launch (start us, length us, event | category | flops | bytes accessed | tf_op | source)
XLA Modules:
  0.0 131.9 jit_solution(11782236532034147897)
XLA Ops:
  0.6 0.7 dynamic-slice_multiply_fusion
  1.4 0.1 add_convert_fusion
  1.4 0.1 convert_element_type.11
  1.5 1.0 fusion
  2.5 0.1 pad_maximum_fusion
  2.6 0.0 copy-start
  2.6 1.6 %copy-done = bf16[1024,1024]{1,0:T(8,128)(2,1)S(1)} copy-done((bf16[1024,1024]{1,0:T(8,128)(2,1)S(1)}, bf16[1024,1024]{1,0:T(8,128)(2,1)}, u32[]{:S(2)}) %copy-start) | copy-done | bytes 2097176
  4.2 1.6 %copy-done.2 = bf16[1024,1024]{1,0:T(8,128)(2,1)S(1)} copy-done((bf16[1024,1024]{1,0:T(8,128)(2,1)S(1)}, bf16[1024,1024]{1,0:T(8,128)(2,1)}, u32[]{:S(2)}) %copy-start.2) | copy-done | bytes 2097176
  5.8 0.9 copy-done.4
  6.7 0.7 copy-done.8
  7.4 40.7 %project_gather.1.kv_ref = bf16[32,2,128,128]{3,2,1,0:T(8,128)(2,1)S(1)} custom-call(bf16[128,1024]{1,0:T(8,128)(2,1)S(1)} %copy-done.4, bf16[1024,1024]{1,0:T(8,128)(2,1)S(1)} %copy-done, bf16[1024,1024]{1,0:T(8,128)(2,1)S(1)} %copy-done.2, f32[8,128]{1,0:T(8,128)S(1)} %bitcast.9, f32[128,128]{1,0:T(8,128)S(1)} %get-tuple-element.23.cos_ref, ...), custom_call_target="tpu_custom_call" | custom-call | tf_op jit(solution)/shard_map/project_gather/pallas_call | solution.py:183
  48.2 0.0 copy-done.6
  48.2 0.0 copy-done.7
  48.2 0.0 copy-done.9
  48.2 0.0 copy-start.1
  48.2 0.0 copy-start.5
  48.2 17.6 %attend.1 = (bf16[128,1024]{1,0:T(8,128)(2,1)}, bf16[2,8,2,2,128,128]{5,4,3,2,1,0:T(8,128)(2,1)S(1)}) custom-call(s32[64]{0:T(128)S(1)} %copy-done.9, bf16[128,1024]{1,0:T(8,128)(2,1)S(1)} %copy-done.6, bf16[128,1024]{1,0:T(8,128)(2,1)S(1)} %copy-done.7, bf16[32,2,128,128]{3,2,1,0:T(8,128)(2,1)S(1)} %project_gather.1.kv_ref), custom_call_target="tpu_custom_call" | custom-call | tf_op jit(solution)/shard_map/attend/pallas_call | solution.py:318
  65.8 1.3 %copy-done.3 = bf16[2,8,2,2,128,128]{5,4,3,2,1,0:T(8,128)(2,1)} copy-done((bf16[2,8,2,2,128,128]{5,4,3,2,1,0:T(8,128)(2,1)}, bf16[2,8,2,2,128,128]{5,4,3,2,1,0:T(8,128)(2,1)S(1)}, u32[]{:S(2)}) %copy-start.3) | copy-done | bytes 2097176
  67.1 0.0 copy-done.1
  67.2 62.7 %finish.1 = (bf16[128,1024]{1,0:T(8,128)(2,1)S(1)}, bf16[64,1024]{1,0:T(8,128)(2,1)S(1)}, f32[8,128]{1,0:T(8,128)S(1)}) custom-call(bf16[128,1024]{1,0:T(8,128)(2,1)S(1)} %copy-done.5, bf16[1024,1024]{1,0:T(8,128)(2,1)S(1)} %copy-done.1, bf16[1024,1024]{1,0:T(8,128)(2,1)} %wv_hbm.1, f32[128,128]{1,0:T(8,128)S(1)} %get-tuple-element.23.cos_ref, ...), custom_call_target="tpu_custom_call" | custom-call | tf_op jit(solution)/shard_map/finish/pallas_call | solution.py:569
  129.9 0.1 constant_dynamic-slice_fusion
  130.0 0.5 slice_bitcast_fusion.2
  130.5 0.7 slice_bitcast_fusion
  131.1 0.7 copy.15
  (8 shorter events, 0.0 us)
Async XLA Ops:
  2.6 1.6 %copy-start = (bf16[1024,1024]{1,0:T(8,128)(2,1)S(1)}, bf16[1024,1024]{1,0:T(8,128)(2,1)}, u32[]{:S(2)}) copy-start(bf16[1024,1024]{1,0:T(8,128)(2,1)} %wk_hbm.1) | copy-start | bytes 6291460
  4.2 1.6 %copy-start.2 = (bf16[1024,1024]{1,0:T(8,128)(2,1)S(1)}, bf16[1024,1024]{1,0:T(8,128)(2,1)}, u32[]{:S(2)}) copy-start(bf16[1024,1024]{1,0:T(8,128)(2,1)} %wv_hbm.1) | copy-start | bytes 6291460
  5.8 0.9 copy-start.4
  6.7 0.7 copy-start.8
  7.4 40.7 %copy-start.6 = (bf16[128,1024]{1,0:T(8,128)(2,1)S(1)}, bf16[128,1024]{1,0:T(8,128)(2,1)}, u32[]{:S(2)}) copy-start(bf16[128,1024]{1,0:T(8,128)(2,1)} %q_ref.1) | copy-start | bytes 786436
  7.4 40.8 %copy-start.7 = (bf16[128,1024]{1,0:T(8,128)(2,1)S(1)}, bf16[128,1024]{1,0:T(8,128)(2,1)}, u32[]{:S(2)}) copy-start(bf16[128,1024]{1,0:T(8,128)(2,1)} %g_ref.1) | copy-start | bytes 786436
  7.4 40.8 %copy-start.9 = (s32[64]{0:T(128)S(1)}, s32[64]{0:T(128)}, u32[]{:S(2)}) copy-start(s32[64]{0:T(128)} %order_ref.1) | copy-start | bytes 772
  48.2 18.9 %copy-start.1 = (bf16[1024,1024]{1,0:T(8,128)(2,1)S(1)}, bf16[1024,1024]{1,0:T(8,128)(2,1)}, u32[]{:S(2)}) copy-start(bf16[1024,1024]{1,0:T(8,128)(2,1)} %wk_hbm.1) | copy-start | bytes 6291460
  48.2 18.9 %copy-start.5 = (bf16[128,1024]{1,0:T(8,128)(2,1)S(1)}, bf16[128,1024]{1,0:T(8,128)(2,1)}, u32[]{:S(2)}) copy-start(bf16[128,1024]{1,0:T(8,128)(2,1)} %x_ref.3) | copy-start | bytes 786436
  65.8 1.3 %copy-start.3 = (bf16[2,8,2,2,128,128]{5,4,3,2,1,0:T(8,128)(2,1)}, bf16[2,8,2,2,128,128]{5,4,3,2,1,0:T(8,128)(2,1)S(1)}, u32[]{:S(2)}) copy-start(bf16[2,8,2,2,128,128]{5,4,3,2,1,0:T(8,128)(2,1)S(1)} %get-tuple-element.11.dkv_ref) | copy-start | bytes 6291460
